TPU v7x, 512 devices: a whole 4x4x16 slice. The times are simulated.
512 devices in a mesh: grp: 4 (over z_hi, core), seq: 128 (over x, y, z_lo).
Axes of the slice: x: 4, y: 4, z: 16 (z_hi: 2, z_lo: 8; z = z_hi * 8 + z_lo), core: 2. Of those that a mesh axis runs over, the one named last changes fastest.
Arguments:
- cand_queries: bfloat16 [4096, 128, 128], P(('grp', 'seq')), may hold values from -256 to 256
- candidate_keys: bfloat16 [512, 128, 128], P(('grp', 'seq')), may hold values from -6 to 6
- candidate_values: bfloat16 [512, 128, 128], P(('grp', 'seq')), may hold values from -24 to 24
- prefix_rotated_keys: bfloat16 [2048, 1024], P(('grp', 'seq')), may hold values from -6.1 to 6.1
- prefix_value_matrix: bfloat16 [2048, 1024], P(('grp', 'seq')), may hold values from -24 to 24
- lengths: int32 [64], replicated, may hold values from 32 to 128
Outputs:
- attended: bfloat16 [4096, 128, 128], P(('grp', 'seq'))
All inputs are finite; a program needn't handle non-finite values.
Results may differ from a plain program's by a relative error of at most 0.0076.
Values may be sent and summed in bfloat16 or wider, within the bound.
A program may use at most 64 MiB of HBM per device.

v0:
```python
import math

import jax
import jax.numpy as jnp
import numpy as np
from jax import lax
from jax.sharding import PartitionSpec as P

QUERY_HEADS = 64
KEY_VALUE_HEADS = 8
HEAD_WIDTH = 128


rope_base = 500000.0


def in_one_piece(arrays, axis, dim, along):
    both = jnp.concatenate(arrays, axis=along)
    filled, at, outs = (lax.all_gather(both, axis, axis=dim, tiled=True), 0, [])
    for a in arrays:
        outs.append(lax.slice_in_dim(filled, at, at + a.shape[along], axis=along))
        at += a.shape[along]
    return tuple(outs)


def rotate(vectors, positions):
    half_width = vectors.shape[-1] // 2
    exponents = jnp.arange(half_width, dtype=jnp.float32) * (2.0 / vectors.shape[-1])
    frequency = 1.0 / jnp.power(jnp.float32(rope_base), exponents)
    angles = positions.astype(jnp.float32)[:, None] * frequency[None, :]
    cosine = jnp.cos(angles)
    sine_table = jnp.sin(angles)
    lower_half = vectors[..., :half_width]
    upper_half = vectors[..., half_width:]
    return jnp.concatenate(
        [
            lower_half * cosine - upper_half * sine_table,
            upper_half * cosine + lower_half * sine_table,
        ],
        axis=-1,
    )


def pick_heads(key_row_list, value_row_list, head_table, sequence_count):
    row_total = key_row_list.shape[0]
    stacked = jnp.stack(
        [
            key_row_list.reshape(row_total, KEY_VALUE_HEADS, HEAD_WIDTH),
            value_row_list.reshape(row_total, KEY_VALUE_HEADS, HEAD_WIDTH),
        ],
        axis=2,
    )
    picked = jnp.take(stacked, head_table, axis=1)
    return picked.reshape(row_total, sequence_count, -1).transpose(1, 0, 2)


def shards(
    cand_queries,
    candidate_keys,
    candidate_values,
    prefix_rotated_keys,
    prefix_value_matrix,
    lengths,
):
    sequence_count = lax.axis_size("seq")
    grp_count = lax.axis_size("grp")
    head_rows = cand_queries.shape[0]
    cand_length = cand_queries.shape[1]
    key_value_rows = candidate_keys.shape[0]
    group_width = QUERY_HEADS // KEY_VALUE_HEADS
    key_value_heads = min(KEY_VALUE_HEADS, key_value_rows)
    prefix_here = prefix_rotated_keys.shape[0]
    prefix_total = prefix_here * sequence_count * grp_count
    score_scale = 1.0 / math.sqrt(HEAD_WIDTH)
    prefix_pick = (
        (np.arange(sequence_count)[:, None] * key_value_rows + np.arange(key_value_heads)[None, :])
        % KEY_VALUE_HEADS
    ).reshape(-1)
    copies = in_one_piece((prefix_rotated_keys, prefix_value_matrix), "grp", 0, 1)
    outgoing = pick_heads(copies[0], copies[1], prefix_pick, sequence_count)
    prefix_pair = lax.all_to_all(outgoing, "seq", split_axis=0, concat_axis=1, tiled=True)
    prefix_pair = prefix_pair.reshape(prefix_total, key_value_heads, 2, HEAD_WIDTH)
    kv_table = np.arange(key_value_rows) % key_value_heads
    prefix_key_rows = jnp.take(prefix_pair[:, :, 0], kv_table, axis=1).transpose(1, 0, 2)
    prefix_value_rows = jnp.take(prefix_pair[:, :, 1], kv_table, axis=1).transpose(1, 0, 2)
    positions = prefix_total + jnp.arange(cand_length, dtype=jnp.int32)
    new_keys = rotate(candidate_keys.astype(jnp.float32), positions).astype(jnp.bfloat16)
    rotated = rotate(cand_queries.astype(jnp.float32), positions).astype(jnp.bfloat16)
    rotated = rotated.reshape(key_value_rows, group_width * cand_length, HEAD_WIDTH)
    all_keys = jnp.concatenate([prefix_key_rows, new_keys], axis=1)
    all_values = jnp.concatenate([prefix_value_rows, candidate_values], axis=1)
    key_count = prefix_total + cand_length
    block_rows = math.gcd(key_count, 512)
    block_count = key_count // block_rows
    row_total = group_width * cand_length
    row_token = jnp.arange(row_total, dtype=jnp.int32) % cand_length
    starts = jnp.arange(block_count, dtype=jnp.int32) * block_rows

    def attend(carry, block):
        maxima, totals, weighted = carry
        block_keys, block_values, first_row = block
        scores = (
            jnp.einsum("krd,knd->krn", rotated, block_keys, preferred_element_type=jnp.float32)
            * score_scale
        )
        cand_offset = first_row + jnp.arange(block_rows, dtype=jnp.int32) - prefix_total
        scores = jnp.where((cand_offset[None, :] <= row_token[:, None])[None], scores, -jnp.inf)
        highest = jnp.maximum(maxima, jnp.max(scores, axis=-1))
        decline = jnp.exp(maxima - highest)
        exponent = jnp.exp(scores - highest[..., None])
        totals = totals * decline + jnp.sum(exponent, axis=-1)
        weighted = weighted * decline[..., None] + jnp.einsum(
            "krn,knd->krd",
            exponent.astype(jnp.bfloat16),
            block_values,
            preferred_element_type=jnp.float32,
        )
        return ((highest, totals, weighted), None)

    start_state = (
        jnp.full((key_value_rows, row_total), -1e30, jnp.float32),
        jnp.zeros((key_value_rows, row_total), jnp.float32),
        jnp.zeros((key_value_rows, row_total, HEAD_WIDTH), jnp.float32),
    )
    key_blocks = all_keys.reshape(key_value_rows, block_count, block_rows, HEAD_WIDTH).transpose(
        1, 0, 2, 3
    )
    value_blocks = all_values.reshape(
        key_value_rows, block_count, block_rows, HEAD_WIDTH
    ).transpose(1, 0, 2, 3)
    final_state, unused = lax.scan(attend, start_state, (key_blocks, value_blocks, starts))
    maxima, totals, weighted = final_state
    attended = (weighted / totals[..., None]).reshape(head_rows, cand_length, HEAD_WIDTH)
    device_place = lax.axis_index("grp") * sequence_count + lax.axis_index("seq")
    cand_of_row = (device_place * head_rows + jnp.arange(head_rows, dtype=jnp.int32)) // QUERY_HEADS
    cand_slots = jnp.arange(lengths.shape[0], dtype=jnp.int32)
    cand_limit = jnp.sum(
        jnp.where(cand_of_row[:, None] == cand_slots[None, :], lengths[None, :], 0), axis=1
    )
    visible = jnp.arange(cand_length, dtype=jnp.int32)[None, :] < cand_limit[:, None]
    return jnp.where(visible[:, :, None], attended, jnp.float32(0.0)).astype(jnp.bfloat16)


def solution(mesh):
    return jax.shard_map(
        shards,
        mesh=mesh,
        in_specs=(
            P(("grp", "seq"), None, None),
            P(("grp", "seq"), None, None),
            P(("grp", "seq"), None, None),
            P(("grp", "seq"), None),
            P(("grp", "seq"), None),
            P(),
        ),
        out_specs=P(("grp", "seq"), None, None),
        check_vma=False,
    )
```

profile of v0, /device:TPU:1, one launch (start us, length us, event | category | flops | bytes accessed | tf_op | source)
XLA Modules:
  0.0 135.4 jit_solution(17232865180039130087)
XLA Ops:
  0.0 0.7 maximum_bitcast_fusion
  0.7 20.7 %all-gather = bf16[4,4,2048]{2,1,0:T(4,128)(2,1)S(1)} all-gather(bf16[1,4,2048]{2,1,0:T(4,128)(2,1)S(1)} %maximum_bitcast_fusion), channel_id=1, replica_groups=mesh['grp'=4,'seq'=128] {'grp'}, dimensions={0}, use_global_device_ids=true | all-gather | bytes 81920 | tf_op jit(solution)/shard_map/all_gather | solution.py:19
  21.5 0.7 pad_clamp_fusion
  22.2 0.8 gather_fusion
  22.9 1.1 copy.33
  24.0 1.7 %copy.34 = bf16[128,16,256]{2,1,0:T(8,128)(2,1)} copy(bf16[128,16,256]{0,2,1:T(8,128)(2,1)S(1)} %bitcast.75) | data formatting | bytes 2097152 | tf_op jit(solution)/shard_map/transpose | solution.py:54
  25.7 14.3 %all-to-all-start = ((bf16[128,16,256]{2,1,0:T(8,128)(2,1)}), bf16[128,16,256]{2,1,0:T(8,128)(2,1)S(1)}, u32[]{:S(2)}, u32[]{:S(2)}) async-start(bf16[128,16,256]{2,1,0:T(8,128)(2,1)} %copy.34), calls=%async_computation | async-start | bytes 2097152 | tf_op jit(solution)/shard_map/all_to_all | solution.py:81
  40.9 0.3 multiply_cosine_fusion
  41.7 52.1 %all-to-all-done = bf16[128,16,256]{2,1,0:T(8,128)(2,1)S(1)} async-done(((bf16[128,16,256]{2,1,0:T(8,128)(2,1)}), bf16[128,16,256]{2,1,0:T(8,128)(2,1)S(1)}, u32[]{:S(2)}, u32[]{:S(2)}) %all-to-all-start) | async-done | bytes 1048608 | tf_op jit(solution)/shard_map/all_to_all | solution.py:81
  94.1 1.5 %fusion.31 = (bf16[2048,1,1,128]{3,2,0,1:T(2,128)(2,1)S(1)}, bf16[2048,1,1,128]{3,2,0,1:T(2,128)(2,1)S(1)}) fusion(bf16[2048,1,2,128]{3,2,0,1:T(2,128)(2,1)S(1)} %reshape.324), kind=kLoop, calls=%fused_computation.69 | loop fusion | bytes 2097152 | tf_op jit(solution)/shard_map/slice | solution.py:85
  95.8 0.7 copy-done.1
  96.6 37.7 %while.17 = (s32[]{:T(128)}, f32[1,1024]{1,0:T(1,128)S(1)}, f32[1,1024]{1,0:T(1,128)S(1)}, f32[1,1024,128]{2,1,0:T(8,128)S(1)}, s32[17]{0:T(128)S(1)}, /*index=5...) while((s32[]{:T(128)}, f32[1,1024]{1,0:T(1,128)S(1)}, ...), condition=%wide.region_4.5_spmd.clone, body=%wide.region_1.4_spmd.clone.sunk | while | flops 68562176 | bytes 3024009 | solution.py:131
  96.6 0.7 dynamic_slice.38
  97.3 0.7 add_add_fusion.2
  98.4 0.4 fusion.45
  98.8 0.7 dynamic_slice.38
  99.5 0.7 add_add_fusion.2
  100.6 0.4 fusion.45
  101.0 0.7 dynamic_slice.38
  101.7 0.7 add_add_fusion.2
  102.8 0.4 fusion.45
  103.2 0.7 dynamic_slice.38
  103.9 0.7 add_add_fusion.2
  105.0 0.4 fusion.45
  105.5 0.7 dynamic_slice.38
  106.1 0.7 add_add_fusion.2
  107.2 0.4 fusion.45
  107.7 0.7 dynamic_slice.38
  108.3 0.7 add_add_fusion.2
  109.4 0.4 fusion.45
  109.9 0.7 dynamic_slice.38
  110.6 0.7 add_add_fusion.2
  111.7 0.4 fusion.45
  112.1 0.7 dynamic_slice.38
  112.8 0.7 add_add_fusion.2
  113.9 0.4 fusion.45
  114.3 0.7 dynamic_slice.38
  115.0 0.7 add_add_fusion.2
  116.1 0.4 fusion.45
  116.5 0.7 dynamic_slice.38
  117.2 0.7 add_add_fusion.2
  118.3 0.4 fusion.45
  118.7 0.7 dynamic_slice.38
  119.4 0.7 add_add_fusion.2
  120.5 0.4 fusion.45
  121.0 0.7 dynamic_slice.38
  121.6 0.7 add_add_fusion.2
  122.7 0.4 fusion.45
  123.2 0.7 dynamic_slice.38
  123.8 0.7 add_add_fusion.2
  125.0 0.4 fusion.45
  125.4 0.7 dynamic_slice.38
  126.1 0.7 add_add_fusion.2
  127.2 0.4 fusion.45
  127.6 0.7 dynamic_slice.38
  128.3 0.7 add_add_fusion.2
  129.4 0.4 fusion.45
  129.8 0.7 dynamic_slice.38
  130.5 0.7 add_add_fusion.2
  131.6 0.4 fusion.45
  132.0 0.7 dynamic_slice.38
  132.7 0.7 add_add_fusion.2
  133.8 0.4 fusion.45
  134.5 0.9 select_convert_fusion
  (138 shorter events, 8.4 us)
Async XLA Ops:
  25.7 14.4 %copy-start = (bf16[8,128,128]{2,1,0:T(8,128)(2,1)S(1)}, bf16[8,128,128]{2,1,0:T(8,128)(2,1)}, u32[]{:S(2)}) copy-start(bf16[8,128,128]{2,1,0:T(8,128)(2,1)} %param.10) | copy-start | bytes 786436
  25.7 14.4 %copy-start.2 = (bf16[1,128,128]{2,1,0:T(8,128)(2,1)S(1)}, bf16[1,128,128]{2,1,0:T(8,128)(2,1)}, u32[]{:S(2)}) copy-start(bf16[1,128,128]{2,1,0:T(8,128)(2,1)} %param.11) | copy-start | bytes 98308
  25.7 68.1 %all-to-all-start = ((bf16[128,16,256]{2,1,0:T(8,128)(2,1)}), bf16[128,16,256]{2,1,0:T(8,128)(2,1)S(1)}, u32[]{:S(2)}, u32[]{:S(2)}) async-start(bf16[128,16,256]{2,1,0:T(8,128)(2,1)} %copy.34), calls=%async_computation | async-start | bytes 2097152 | tf_op jit(solution)/shard_map/all_to_all | solution.py:81
  40.1 0.7 copy-start.3
  95.8 0.8 copy-start.1
where the time goes:
time: 136 us; the launch traced here: 135 us
  waiting for transfers between devices  52.1 us (38%)
  blocking collectives  20.7 us (15%)
  other arithmetic  17.9 us (13%)
  local copies, waits for them, and re-layouts  17.9 us (13%)
  starting transfers between devices  14.3 us (11%)
  matrix products  11.1 us (8%)
    all_to_all x1, waiting for transfers between devices, shards(): lax.all_to_all(outgoing, 'seq', split_axis=0, concat_axis=1, tiled=True)  52.1 us
    all_gather x1, blocking collectives, in_one_piece(): filled, at, outs = (lax.all_gather(both, axis, axis=dim, tiled=True), 0, [])  20.7 us
    all_to_all x1, starting transfers between devices, shards(): lax.all_to_all(outgoing, 'seq', split_axis=0, concat_axis=1, tiled=True)  14.3 us
    sub x17, other arithmetic, attend(): first_row + jnp.arange(block_rows, dtype=jnp.int32) - prefix_total  11.8 us
    dynamic_slice x17, local copies, waits for them, and re-layouts, shards(): lax.scan(attend, start_state, (key_blocks, value_blocks, starts))  11.3 us
    dot_general x17, matrix products, attend(): jnp.einsum('krn,knd->krd', exponent.astype(jnp.bfloat16), block_values, p...  6.91 us
    dot_general x17, matrix products, attend(): jnp.einsum('krd,knd->krn', rotated, block_keys, preferred_element_type=jn...  4.16 us
  transfers between devices with their start and end apart: 1, of which 1 were waited for; matrix products, arithmetic and copies ran while one was open for 1% of the time, Pallas kernels for 0%

commit v1 on v0

v1 whole, which is shorter than its diff:
```python
import functools
import math

import jax
import jax.numpy as jnp
import numpy as np
from jax import lax
from jax.experimental import pallas as pl
from jax.experimental.pallas import tpu as pltpu
from jax.sharding import PartitionSpec as P

QUERY_HEADS = 64
KEY_VALUE_HEADS = 8
HEAD_WIDTH = 128
SLOTS = 128
PREFIX = 2048
ROPE_BASE = 500000.0
GROUP = QUERY_HEADS // KEY_VALUE_HEADS
ROWS = GROUP * SLOTS
SCALE2 = math.log2(math.e) / math.sqrt(HEAD_WIDTH)

NX, NY, NZ, ZL = 4, 4, 16, 8
MESH = pl.DeviceIdType.MESH
BLOCK = 256


def rotation_table():
    half = HEAD_WIDTH // 2
    exponents = np.arange(half, dtype=np.float32) * np.float32(2.0 / HEAD_WIDTH)
    frequency = (np.float32(1.0) / np.power(np.float32(ROPE_BASE), exponents)).astype(np.float32)
    positions = np.float32(PREFIX) + np.arange(SLOTS, dtype=np.float32)
    angles = (positions[:, None] * frequency[None, :]).astype(np.float32).astype(np.float64)
    return np.concatenate([np.cos(angles), np.sin(angles)], axis=1).astype(np.float32)


def device(x, y, z, core):
    return ((z // ZL) * 2 + core, (x * NY + y) * ZL + z % ZL)


def kernel(
    kp_hbm, vp_hbm, q_hbm, ck_hbm, cv_hbm, table_hbm, len_ref, out_ref,
    kp, vp, q, ck, cv, table, send, landed, kv0, kv1, acc, top,
    in_sem, a_send, a_recv, s1_send, s1_recv, s2_send, s2_recv, d_send, d_recv,
):
    grp, seq = lax.axis_index("grp"), lax.axis_index("seq")
    core, zh = grp % 2, grp // 2
    z = zh * ZL + seq % ZL
    y = (seq // ZL) % NY
    x = seq // (ZL * NY)

    loads = [
        pltpu.make_async_copy(s, d, in_sem.at[i])
        for i, (s, d) in enumerate(
            [(kp_hbm, kp), (vp_hbm, vp), (q_hbm, q), (ck_hbm, ck), (cv_hbm, cv), (table_hbm, table)]
        )
    ]
    for load in loads:
        load.start()

    barrier = pltpu.get_barrier_semaphore()
    far = [8, 7, 9, 6, 10, 5, 11, 4, 12, 3, 13, 2, 14, 1, 15]
    near = [1, 3, 2]
    for d in far:
        pl.semaphore_signal(barrier, inc=1, device_id=device(x, y, (z + d) % NZ, core), device_id_type=MESH)
    for d in near:
        pl.semaphore_signal(barrier, inc=1, device_id=device((x + d) % NX, y, z, core), device_id_type=MESH)
        pl.semaphore_signal(barrier, inc=1, device_id=device(x, (y + d) % NY, z, core), device_id_type=MESH)
    pl.semaphore_signal(barrier, inc=1, device_id=device(x, y, z, 1 - core), device_id_type=MESH)

    loads[0].wait()
    loads[1].wait()
    both = jnp.concatenate([kp[...].astype(jnp.float32), vp[...].astype(jnp.float32)], axis=0)
    both = both.astype(jnp.bfloat16)
    for h in range(KEY_VALUE_HEADS):
        send[h] = both[:, h * HEAD_WIDTH : (h + 1) * HEAD_WIDTH]

    pl.semaphore_wait(barrier, len(far) + 2 * len(near) + 1)

    for d in far:
        zt = (z + d) % NZ
        pltpu.make_async_remote_copy(
            src_ref=send.at[zt % ZL], dst_ref=landed.at[z], send_sem=a_send, recv_sem=a_recv,
            device_id=device(x, y, zt, core), device_id_type=MESH,
        ).start()
    pltpu.make_async_copy(send.at[z % ZL], landed.at[z], a_recv).start()

    for load in loads[2:]:
        load.wait()
    lower = lax.broadcasted_iota(jnp.int32, (SLOTS, HEAD_WIDTH), 1) < HEAD_WIDTH // 2
    cs = table[...]
    turned = pltpu.roll(cs, HEAD_WIDTH // 2, 1)
    cosine = jnp.where(lower, cs, turned)
    sine = jnp.where(lower, -turned, cs)

    def rotate(rows):
        rows = rows.astype(jnp.float32)
        return (rows * cosine + pltpu.roll(rows, HEAD_WIDTH // 2, 1) * sine).astype(jnp.bfloat16)

    new_keys = rotate(ck[...].reshape(SLOTS, HEAD_WIDTH))
    new_values = cv[...].reshape(SLOTS, HEAD_WIDTH)
    ones = jnp.ones((SLOTS, HEAD_WIDTH), jnp.bfloat16)
    new_values = jnp.concatenate([new_values, ones], axis=1)
    causal = lax.broadcasted_iota(jnp.int32, (SLOTS, SLOTS), 1) <= lax.broadcasted_iota(
        jnp.int32, (SLOTS, SLOTS), 0
    )

    def own(h, carry):
        rows = rotate(q[h])
        q[h] = rows
        s = lax.dot_general(rows, new_keys, (((1,), (1,)), ((), ())), preferred_element_type=jnp.float32)
        s = jnp.where(causal, s * SCALE2, -jnp.inf)
        m = jnp.max(s, axis=1, keepdims=True)
        p = jnp.exp2(s - m).astype(jnp.bfloat16)
        r = pl.ds(pl.multiple_of(h * SLOTS, SLOTS), SLOTS)
        acc[r, :] = jnp.dot(p, new_values, preferred_element_type=jnp.float32)
        top[r, :] = jnp.broadcast_to(m, (SLOTS, HEAD_WIDTH))
        return carry

    lax.fori_loop(0, GROUP, own, 0)

    pltpu.make_async_copy(landed, landed, a_recv).wait()
    first = lax.broadcasted_iota(jnp.int32, (8, HEAD_WIDTH), 0) < 4
    for half, ref, a, b in ((0, kv0, y, x), (1, kv1, x, y)):
        keys, values = [], []
        for i in range(half * NZ // 2, (half + 1) * NZ // 2, 2):
            even, odd = landed[i].astype(jnp.float32), landed[i + 1].astype(jnp.float32)
            keys.append(jnp.where(first, even, pltpu.roll(odd, 4, 0)))
            values.append(jnp.where(first, pltpu.roll(even, 4, 0), odd))
        ref[core, a, b, 0] = jnp.concatenate(keys, axis=0).astype(jnp.bfloat16)
        ref[core, a, b, 1] = jnp.concatenate(values, axis=0).astype(jnp.bfloat16)

    for d in near:
        pltpu.make_async_remote_copy(
            src_ref=kv0.at[core, y, x], dst_ref=kv0.at[core, y, x], send_sem=s1_send.at[0],
            recv_sem=s1_recv.at[0], device_id=device((x + d) % NX, y, z, core), device_id_type=MESH,
        ).start()
        pltpu.make_async_remote_copy(
            src_ref=kv1.at[core, x, y], dst_ref=kv1.at[core, x, y], send_sem=s1_send.at[1],
            recv_sem=s1_recv.at[1], device_id=device(x, (y + d) % NY, z, core), device_id_type=MESH,
        ).start()
    three = kv0.at[0, 0, pl.ds(0, 3)]
    pltpu.make_async_copy(three, three, s1_recv.at[0]).wait()
    pltpu.make_async_copy(three, three, s1_recv.at[1]).wait()
    for d in near:
        pltpu.make_async_remote_copy(
            src_ref=kv0.at[core, y], dst_ref=kv0.at[core, y], send_sem=s2_send.at[0],
            recv_sem=s2_recv.at[0, d - 1], device_id=device(x, (y + d) % NY, z, core), device_id_type=MESH,
        ).start()
        pltpu.make_async_remote_copy(
            src_ref=kv1.at[core, x], dst_ref=kv1.at[core, x], send_sem=s2_send.at[1],
            recv_sem=s2_recv.at[1, d - 1], device_id=device((x + d) % NX, y, z, core), device_id_type=MESH,
        ).start()

    def across(slot, yy, xx):
        for i, ref, line in ((0, kv0, yy), (1, kv1, xx)):
            pltpu.make_async_remote_copy(
                src_ref=ref.at[core, line], dst_ref=ref.at[core, line], send_sem=d_send.at[i],
                recv_sem=d_recv.at[i, slot], device_id=device(x, y, z, 1 - core), device_id_type=MESH,
            ).start()

    line = kv0.at[0, 0]

    def line_wait(sems, slot):
        for i in (0, 1):
            pltpu.make_async_copy(line, line, sems.at[i, slot]).wait()

    ones_block = jnp.ones((SLOTS, HEAD_WIDTH), jnp.bfloat16)

    def attend(parts, last=False):
        def rows_of(ref, c, l, which):
            return ref[c, l, :, which].reshape(SLOTS, HEAD_WIDTH)

        def body(i, carry):
            r = pl.ds(pl.multiple_of(i * BLOCK, BLOCK), BLOCK)
            heads = BLOCK // SLOTS
            rows = q[pl.ds(i * heads, heads)].reshape(BLOCK, HEAD_WIDTH)
            keys = jnp.concatenate([rows_of(ref, c, l, 0) for ref, c, l in parts], axis=0)
            values = jnp.concatenate(
                [jnp.concatenate([rows_of(ref, c, l, 1), ones_block], axis=1) for ref, c, l in parts], axis=0
            )
            s = lax.dot_general(rows, keys, (((1,), (1,)), ((), ())), preferred_element_type=jnp.float32)
            s = s * SCALE2
            old = top[r, :]
            m = jnp.maximum(old, jnp.max(s, axis=1, keepdims=True))
            decline = jnp.exp2(old - m)
            p = jnp.exp2(s - m[:, :1]).astype(jnp.bfloat16)
            o = acc[r, :] * jnp.concatenate([decline, decline], axis=1) + jnp.dot(
                p, values, preferred_element_type=jnp.float32
            )
            if not last:
                acc[r, :] = o
                top[r, :] = m
            else:
                mine = (grp * lax.axis_size("seq") + seq) // KEY_VALUE_HEADS
                token = lax.broadcasted_iota(jnp.int32, (BLOCK, HEAD_WIDTH), 0) % SLOTS
                result = jnp.where(token < len_ref[mine], o[:, :HEAD_WIDTH] / o[:, HEAD_WIDTH:], 0.0)
                out_ref[pl.ds(i * heads, heads)] = result.astype(jnp.bfloat16).reshape(heads, SLOTS, HEAD_WIDTH)
            return carry

        lax.fori_loop(0, ROWS // BLOCK, body, 0)

    def lines(c, yy, xx):
        return [(kv0, c, yy), (kv1, c, xx)]

    across(0, y, x)
    attend(lines(core, y, x))
    before = (0, y, x)
    for d in near:
        yy, xx = (y + NY - d) % NY, (x + NX - d) % NX
        line_wait(s2_recv, d - 1)
        across(d, yy, xx)
        line_wait(d_recv, before[0])
        attend(lines(1 - core, before[1], before[2]) + lines(core, yy, xx))
        before = (d, yy, xx)
    line_wait(d_recv, before[0])
    attend(lines(1 - core, before[1], before[2]), last=True)

    pltpu.make_async_copy(landed.at[pl.ds(0, NZ - 1)], landed.at[pl.ds(0, NZ - 1)], a_send).wait()
    lines3 = kv0.at[0, pl.ds(0, 3)]
    for i in (0, 1):
        pltpu.make_async_copy(three, three, s1_send.at[i]).wait()
        pltpu.make_async_copy(lines3, lines3, s2_send.at[i]).wait()
        pltpu.make_async_copy(kv0.at[0], kv0.at[0], d_send.at[i]).wait()


def shards(cand_queries, candidate_keys, candidate_values, prefix_keys, prefix_values, lengths):
    bf16, f32 = jnp.bfloat16, jnp.float32
    anywhere = pl.BlockSpec(memory_space=pl.ANY)
    dma = pltpu.SemaphoreType.DMA
    return pl.pallas_call(
        kernel,
        out_shape=jax.ShapeDtypeStruct(cand_queries.shape, bf16),
        in_specs=[anywhere] * 6 + [pl.BlockSpec(memory_space=pltpu.SMEM)],
        out_specs=pl.BlockSpec(memory_space=pltpu.VMEM),
        scratch_shapes=[
            pltpu.VMEM(prefix_keys.shape, bf16),
            pltpu.VMEM(prefix_values.shape, bf16),
            pltpu.VMEM(cand_queries.shape, bf16),
            pltpu.VMEM(candidate_keys.shape, bf16),
            pltpu.VMEM(candidate_values.shape, bf16),
            pltpu.VMEM((SLOTS, HEAD_WIDTH), f32),
            pltpu.VMEM((KEY_VALUE_HEADS, 8, HEAD_WIDTH), bf16),
            pltpu.VMEM((NZ, 8, HEAD_WIDTH), bf16),
            pltpu.VMEM((2, NY, NX, 2, 32, HEAD_WIDTH), bf16),
            pltpu.VMEM((2, NX, NY, 2, 32, HEAD_WIDTH), bf16),
            pltpu.VMEM((ROWS, 2 * HEAD_WIDTH), f32),
            pltpu.VMEM((ROWS, HEAD_WIDTH), f32),
            dma((6,)),
            dma,
            dma,
            dma((2,)),
            dma((2,)),
            dma((2,)),
            dma((2, 3)),
            dma((2,)),
            dma((2, 4)),
        ],
        compiler_params=pltpu.CompilerParams(
            collective_id=0, has_side_effects=True, vmem_limit_bytes=40 * 1024 * 1024
        ),
    )(prefix_keys, prefix_values, cand_queries, candidate_keys, candidate_values, jnp.asarray(rotation_table()), lengths)


def solution(mesh):
    split = P(("grp", "seq"), None, None)
    rows = P(("grp", "seq"), None)
    return jax.shard_map(
        shards,
        mesh=mesh,
        in_specs=(split, split, split, rows, rows, P()),
        out_specs=split,
        check_vma=False,
    )
```

time: 136 us -> 47.8 us (0.35)
  waiting for transfers between devices: 52.1 us -> 0 us
  Pallas kernels: 0 us -> 41.3 us
  blocking collectives: 20.7 us -> 0 us
  other arithmetic: 17.9 us -> 0 us
  starting transfers between devices: 14.3 us -> 0 us
  local copies, waits for them, and re-layouts: 17.9 us -> 6.06 us
  matrix products: 11.1 us -> 0 us
    all_to_all x1 -> x0, waiting for transfers between devices: 52.1 us -> none  [shards(): lax.all_to_all(outgoing, 'seq', split_axis=0, concat_axis=1, tiled=True)]
    pallas_call x0 -> x1, Pallas kernels: none -> 41.3 us  [shards(): pl.pallas_call(kernel, out_shape=jax.ShapeDtypeStruct(cand_queries.shape,...]
    all_gather x1 -> x0, blocking collectives: 20.7 us -> none  [in_one_piece(): filled, at, outs = (lax.all_gather(both, axis, axis=dim, tiled=True), 0, [])]
    all_to_all x1 -> x0, starting transfers between devices: 14.3 us -> none  [shards(): lax.all_to_all(outgoing, 'seq', split_axis=0, concat_axis=1, tiled=True)]
    sub x17 -> x0, other arithmetic: 11.8 us -> none  [attend(): first_row + jnp.arange(block_rows, dtype=jnp.int32) - prefix_total]
    dynamic_slice x17 -> x0, local copies, waits for them, and re-layouts: 11.3 us -> none  [shards(): lax.scan(attend, start_state, (key_blocks, value_blocks, starts))]
    dot_general x34 -> x0, matrix products: 11.1 us -> none  [the longest x17 6.91 us: attend(): jnp.einsum('krn,knd->krd', exponent.astype(jnp.bfloat16), block_values, p...]
    unnamed x14 -> x15, local copies, waits for them, and re-layouts: 1.03 us -> 6.06 us
  transfers between devices with their start and end apart: 1 -> 0, of which waited for: 1 -> 0; matrix products, arithmetic and copies ran while one was open for 1% -> 0% of each run, Pallas kernels for 0% -> 0%
where the time goes in v1:
time: 47.8 us; the launch traced here: 47.4 us
  Pallas kernels  41.3 us (86%)
  local copies, waits for them, and re-layouts  6.06 us (13%)
    pallas_call x1, Pallas kernels, shards(): pl.pallas_call(kernel, out_shape=jax.ShapeDtypeStruct(cand_queries.shape,...  41.3 us
    unnamed x15, local copies, waits for them, and re-layouts  6.06 us

profile of v1, /device:TPU:1, one launch (start us, length us, event | category | flops | bytes accessed | tf_op | source)
XLA Modules:
  0.0 47.4 jit_solution(3143795660168435342)
XLA Ops:
  0.0 0.0 copy-start
  0.0 0.9 %copy-done = bf16[8,128,128]{2,1,0:T(8,128)(2,1)S(1)} copy-done((bf16[8,128,128]{2,1,0:T(8,128)(2,1)S(1)}, bf16[8,128,128]{2,1,0:T(8,128)(2,1)}, u32[]{:S(2)}) %copy-start) | copy-done | bytes 262168
  1.0 0.0 copy-start.1
  1.0 0.8 %copy-done.1 = f32[128,128]{1,0:T(8,128)S(1)} copy-done((f32[128,128]{1,0:T(8,128)S(1)}, f32[128,128]{1,0:T(8,128)}, u32[]{:S(2)}) %copy-start.1) | copy-done | bytes 65560
  1.8 0.0 copy-start.2
  1.8 0.8 %copy-done.2 = bf16[1,128,128]{2,1,0:T(8,128)(2,1)S(1)} copy-done((bf16[1,128,128]{2,1,0:T(8,128)(2,1)S(1)}, bf16[1,128,128]{2,1,0:T(8,128)(2,1)}, u32[]{:S(2)}) %copy-start.2) | copy-done | bytes 32792
  2.5 0.0 copy-start.3
  2.6 0.8 %copy-done.3 = bf16[1,128,128]{2,1,0:T(8,128)(2,1)S(1)} copy-done((bf16[1,128,128]{2,1,0:T(8,128)(2,1)S(1)}, bf16[1,128,128]{2,1,0:T(8,128)(2,1)}, u32[]{:S(2)}) %copy-start.3) | copy-done | bytes 32792
  3.3 0.0 copy-start.4
  3.3 0.7 %copy-done.4 = bf16[4,1024]{1,0:T(4,128)(2,1)S(1)} copy-done((bf16[4,1024]{1,0:T(4,128)(2,1)S(1)}, bf16[4,1024]{1,0:T(4,128)(2,1)}, u32[]{:S(2)}) %copy-start.4) | copy-done | bytes 8216
  4.0 0.0 copy-start.5
  4.0 0.7 %copy-done.5 = bf16[4,1024]{1,0:T(4,128)(2,1)S(1)} copy-done((bf16[4,1024]{1,0:T(4,128)(2,1)S(1)}, bf16[4,1024]{1,0:T(4,128)(2,1)}, u32[]{:S(2)}) %copy-start.5) | copy-done | bytes 8216
  4.7 0.0 copy-start.6
  4.7 0.7 %copy-done.6 = s32[64]{0:T(128)S(1)} copy-done((s32[64]{0:T(128)S(1)}, s32[64]{0:T(128)}, u32[]{:S(2)}) %copy-start.6) | copy-done | bytes 280
  5.4 41.3 %shard_map.73 = bf16[8,128,128]{2,1,0:T(8,128)(2,1)S(1)} custom-call(bf16[4,1024]{1,0:T(4,128)(2,1)S(1)} %copy-done.4, bf16[4,1024]{1,0:T(4,128)(2,1)S(1)} %copy-done.5, bf16[8,128,128]{2,1,0:T(8,128)(2,1)S(1)} %copy-done, bf16[1,128,128]{2,1,0:T(8,128)(2,1)S(1)} %copy-done.2, bf16[1,128,128]{2,1,0:T(8,128)(2,1)S(1)} %copy-done.3, f32[128,128]{1,0:T(8,128)S(1)} %copy-done.1, ...), custom_call_target="tpu_custom_call" | custom-call | tf_op jit(solution)/shard_map/pallas_call | solution.py:230
  46.7 0.7 %copy.9 = bf16[8,128,128]{2,1,0:T(8,128)(2,1)} copy(bf16[8,128,128]{2,1,0:T(8,128)(2,1)S(1)} %shard_map.73) | data formatting | bytes 524288
Async XLA Ops:
  0.0 0.9 %copy-start = (bf16[8,128,128]{2,1,0:T(8,128)(2,1)S(1)}, bf16[8,128,128]{2,1,0:T(8,128)(2,1)}, u32[]{:S(2)}) copy-start(bf16[8,128,128]{2,1,0:T(8,128)(2,1)} %q_hbm.1) | copy-start | bytes 786436
  1.0 0.8 %copy-start.1 = (f32[128,128]{1,0:T(8,128)S(1)}, f32[128,128]{1,0:T(8,128)}, u32[]{:S(2)}) copy-start(f32[128,128]{1,0:T(8,128)} %constant.2.clone.table_hbm) | copy-start | bytes 196612
  1.8 0.8 %copy-start.2 = (bf16[1,128,128]{2,1,0:T(8,128)(2,1)S(1)}, bf16[1,128,128]{2,1,0:T(8,128)(2,1)}, u32[]{:S(2)}) copy-start(bf16[1,128,128]{2,1,0:T(8,128)(2,1)} %ck_hbm.1) | copy-start | bytes 98308
  2.5 0.8 %copy-start.3 = (bf16[1,128,128]{2,1,0:T(8,128)(2,1)S(1)}, bf16[1,128,128]{2,1,0:T(8,128)(2,1)}, u32[]{:S(2)}) copy-start(bf16[1,128,128]{2,1,0:T(8,128)(2,1)} %cv_hbm.1) | copy-start | bytes 98308
  3.3 0.7 %copy-start.4 = (bf16[4,1024]{1,0:T(4,128)(2,1)S(1)}, bf16[4,1024]{1,0:T(4,128)(2,1)}, u32[]{:S(2)}) copy-start(bf16[4,1024]{1,0:T(4,128)(2,1)} %kp_hbm.1) | copy-start | bytes 24580
  4.0 0.7 %copy-start.5 = (bf16[4,1024]{1,0:T(4,128)(2,1)S(1)}, bf16[4,1024]{1,0:T(4,128)(2,1)}, u32[]{:S(2)}) copy-start(bf16[4,1024]{1,0:T(4,128)(2,1)} %vp_hbm.1) | copy-start | bytes 24580
  4.7 0.7 %copy-start.6 = (s32[64]{0:T(128)S(1)}, s32[64]{0:T(128)}, u32[]{:S(2)}) copy-start(s32[64]{0:T(128)} %len_ref.1) | copy-start | bytes 772

commit v2 on v1

v2 whole, which is shorter than its diff:
```python
import functools
import math

import jax
import jax.numpy as jnp
import numpy as np
from jax import lax
from jax.experimental import pallas as pl
from jax.experimental.pallas import tpu as pltpu
from jax.sharding import PartitionSpec as P

QUERY_HEADS = 64
KEY_VALUE_HEADS = 8
HEAD_WIDTH = 128
SLOTS = 128
PREFIX = 2048
ROPE_BASE = 500000.0
GROUP = QUERY_HEADS // KEY_VALUE_HEADS
ROWS = GROUP * SLOTS
SCALE2 = math.log2(math.e) / math.sqrt(HEAD_WIDTH)

NX, NY, NZ, ZL = 4, 4, 16, 8
MESH = pl.DeviceIdType.MESH
BLOCK = 256
WAVES = 2
EARLY, LATE = 4, 8
PER = NZ // WAVES
OFFSETS = sorted(
    [(dx, dy) for dx in range(NX) for dy in range(NY)],
    key=lambda o: min(o[0], NX - o[0]) + min(o[1], NY - o[1]),
)
SET = 8
SETS = NX * NY // SET


def rotation_table():
    half = HEAD_WIDTH // 2
    exponents = np.arange(half, dtype=np.float32) * np.float32(2.0 / HEAD_WIDTH)
    frequency = (np.float32(1.0) / np.power(np.float32(ROPE_BASE), exponents)).astype(np.float32)
    positions = np.float32(PREFIX) + np.arange(SLOTS, dtype=np.float32)
    angles = (positions[:, None] * frequency[None, :]).astype(np.float32).astype(np.float64)
    return np.concatenate([np.cos(angles), np.sin(angles)], axis=1).astype(np.float32)


def device(x, y, z, core):
    return ((z // ZL) * 2 + core, (x * NY + y) * ZL + z % ZL)


def kernel(
    kp_hbm, vp_hbm, q_hbm, ck_hbm, cv_hbm, table_hbm, len_ref, out_ref,
    kp, vp, q, ck, cv, table, send, landed, kv, acc, top,
    in_sem, a_send, a_recv, p_send, p_recv, d_send, d_recv, ready, late_in, all_in,
):
    grp, seq = lax.axis_index("grp"), lax.axis_index("seq")
    core, zh = grp % 2, grp // 2
    z = zh * ZL + seq % ZL
    y = (seq // ZL) % NY
    x = seq // (ZL * NY)

    loads = [
        pltpu.make_async_copy(s, d, in_sem.at[i])
        for i, (s, d) in enumerate(
            [(kp_hbm, kp), (vp_hbm, vp), (q_hbm, q), (ck_hbm, ck), (cv_hbm, cv), (table_hbm, table)]
        )
    ]
    for load in loads:
        load.start()

    barrier = pltpu.get_barrier_semaphore()
    early, late = z < EARLY, z >= LATE

    def signal(sem, *place):
        pl.semaphore_signal(sem, inc=1, device_id=device(*place), device_id_type=MESH)

    for zt in range(NZ):

        @pl.when(early & (z != zt))
        def _():
            signal(barrier, x, y, zt, 1)

    @pl.when(core == 0)
    def _():
        signal(barrier, x, y, z, 1)

    loads[0].wait()
    loads[1].wait()
    both = jnp.concatenate([kp[...].astype(jnp.float32), vp[...].astype(jnp.float32)], axis=0)
    both = both.astype(jnp.bfloat16)
    for h in range(KEY_VALUE_HEADS):
        send[h] = both[:, h * HEAD_WIDTH : (h + 1) * HEAD_WIDTH]

    @pl.when(core == 1)
    def _():
        pl.semaphore_wait(barrier, jnp.where(early, 2 * EARLY - 1, 2 * EARLY + 1))
        signal(ready, x, y, z, 0)

    @pl.when(core == 0)
    def _():
        pl.semaphore_wait(ready, 1)

    def give(zt):
        pltpu.make_async_remote_copy(
            src_ref=send.at[zt % ZL], dst_ref=landed.at[z], send_sem=a_send, recv_sem=a_recv.at[z // PER],
            device_id=device(x, y, zt, core), device_id_type=MESH,
        ).start()

    for zt in range(EARLY):

        @pl.when(z != zt)
        def _():
            give(zt)

        @pl.when(late)
        def _():
            signal(late_in, x, y, zt, core)

    @pl.when(core == 0)
    def _():
        for dx, dy in OFFSETS[:0:-1]:
            signal(barrier, (x + dx) % NX, (y + dy) % NY, z, 0)
        for zt in range(NZ):
            far_end = z != zt
            if zt < EARLY:
                far_end &= ~late

            @pl.when(far_end & ~early)
            def _():
                signal(barrier, x, y, zt, 0)

    for load in loads[2:]:
        load.wait()
    lower = lax.broadcasted_iota(jnp.int32, (SLOTS, HEAD_WIDTH), 1) < HEAD_WIDTH // 2
    cs = table[...]
    turned = pltpu.roll(cs, HEAD_WIDTH // 2, 1)
    cosine = jnp.where(lower, cs, turned)
    sine = jnp.where(lower, -turned, cs)

    def rotate(rows):
        rows = rows.astype(jnp.float32)
        return (rows * cosine + pltpu.roll(rows, HEAD_WIDTH // 2, 1) * sine).astype(jnp.bfloat16)

    new_keys = rotate(ck[...].reshape(SLOTS, HEAD_WIDTH))
    new_values = cv[...].reshape(SLOTS, HEAD_WIDTH)
    ones = jnp.ones((SLOTS, HEAD_WIDTH), jnp.bfloat16)
    new_values = jnp.concatenate([new_values, ones], axis=1)
    causal = lax.broadcasted_iota(jnp.int32, (SLOTS, SLOTS), 1) <= lax.broadcasted_iota(
        jnp.int32, (SLOTS, SLOTS), 0
    )

    def own(h, carry):
        rows = rotate(q[h])
        q[h] = rows
        s = lax.dot_general(rows, new_keys, (((1,), (1,)), ((), ())), preferred_element_type=jnp.float32)
        s = jnp.where(causal, s * SCALE2, -jnp.inf)
        m = jnp.max(s, axis=1, keepdims=True)
        p = jnp.exp2(s - m).astype(jnp.bfloat16)
        r = pl.ds(pl.multiple_of(h * SLOTS, SLOTS), SLOTS)
        acc[r, :] = jnp.dot(p, new_values, preferred_element_type=jnp.float32)
        top[r, :] = jnp.broadcast_to(m, (SLOTS, HEAD_WIDTH))
        return carry

    lax.fori_loop(0, GROUP, own, 0)

    @pl.when(core == 0)
    def _():
        plane, middle = NX * NY - 1, LATE - EARLY
        others = jnp.where(early, middle, NZ - EARLY - 1)
        pl.semaphore_wait(barrier, plane + others)
        signal(all_in, x, y, z, 1)

    @pl.when(core == 1)
    def _():
        pl.semaphore_wait(all_in, 1)

    for zt in range(EARLY, NZ):
        there = z != zt
        if zt >= LATE:
            there &= ~early

        @pl.when(there)
        def _():
            give(zt)

    pltpu.make_async_copy(send.at[z % ZL], landed.at[z], a_recv.at[z // PER]).start()

    half_line = lax.broadcasted_iota(jnp.int32, (8, HEAD_WIDTH), 0) < 4
    for w in range(WAVES):
        src = (z // PER + w) % WAVES
        arrived = landed.at[pl.ds(src * PER, PER)]
        pltpu.make_async_copy(arrived, arrived, a_recv.at[src]).wait()
        keys, values = [], []
        for i in range(0, PER, 2):
            even = landed[src * PER + i].astype(jnp.float32)
            odd = landed[src * PER + i + 1].astype(jnp.float32)
            keys.append(jnp.where(half_line, even, pltpu.roll(odd, 4, 0)))
            values.append(jnp.where(half_line, pltpu.roll(even, 4, 0), odd))
        kv[w, core, 0, 0] = jnp.concatenate(keys, axis=0).astype(jnp.bfloat16)
        kv[w, core, 0, 1] = jnp.concatenate(values, axis=0).astype(jnp.bfloat16)
        for i, (dx, dy) in enumerate(OFFSETS):
            if i:
                pltpu.make_async_remote_copy(
                    src_ref=kv.at[w, core, 0], dst_ref=kv.at[w, core, i], send_sem=p_send.at[w],
                    recv_sem=p_recv.at[w, i // SET], device_id=device((x + dx) % NX, (y + dy) % NY, z, core),
                    device_id_type=MESH,
                ).start()

        if w == 0:

            @pl.when(early)
            def _():
                pl.semaphore_wait(late_in, NZ - LATE)
                for zt in range(LATE, NZ):
                    give(zt)

    ones_block = jnp.ones((SET * PER * 4, HEAD_WIDTH), jnp.bfloat16)
    mine = (grp * lax.axis_size("seq") + seq) // KEY_VALUE_HEADS

    def attend(parts, last=False):
        def rows_of(w, c, g, which):
            return kv[w, c, g * SET : (g + 1) * SET, which].reshape(SET * PER * 4, HEAD_WIDTH)

        def body(i, carry):
            r = pl.ds(pl.multiple_of(i * BLOCK, BLOCK), BLOCK)
            heads = BLOCK // SLOTS
            rows = q[pl.ds(i * heads, heads)].reshape(BLOCK, HEAD_WIDTH)
            keys = jnp.concatenate([rows_of(*p, 0) for p in parts], axis=0)
            values = jnp.concatenate(
                [jnp.concatenate([rows_of(*p, 1), ones_block], axis=1) for p in parts], axis=0
            )
            s = lax.dot_general(rows, keys, (((1,), (1,)), ((), ())), preferred_element_type=jnp.float32)
            s = s * SCALE2
            old = top[r, :]
            m = jnp.maximum(old, jnp.max(s, axis=1, keepdims=True))
            decline = jnp.exp2(old - m)
            p = jnp.exp2(s - m[:, :1]).astype(jnp.bfloat16)
            o = acc[r, :] * jnp.concatenate([decline, decline], axis=1) + jnp.dot(
                p, values, preferred_element_type=jnp.float32
            )
            if not last:
                acc[r, :] = o
                top[r, :] = m
            else:
                token = lax.broadcasted_iota(jnp.int32, (BLOCK, HEAD_WIDTH), 0) % SLOTS
                result = jnp.where(token < len_ref[mine], o[:, :HEAD_WIDTH] / o[:, HEAD_WIDTH:], 0.0)
                out_ref[pl.ds(i * heads, heads)] = result.astype(jnp.bfloat16).reshape(heads, SLOTS, HEAD_WIDTH)
            return carry

        lax.fori_loop(0, ROWS // BLOCK, body, 0)

    before = None
    for w in range(WAVES):
        for g in range(SETS):
            whole = kv.at[w, core, pl.ds(g * SET, SET)]
            if g:
                pltpu.make_async_copy(whole, whole, p_recv.at[w, g]).wait()
            else:
                rest = kv.at[w, core, pl.ds(1, SET - 1)]
                pltpu.make_async_copy(rest, rest, p_recv.at[w, g]).wait()
            pltpu.make_async_remote_copy(
                src_ref=whole, dst_ref=whole, send_sem=d_send, recv_sem=d_recv.at[w, g],
                device_id=device(x, y, z, 1 - core), device_id_type=MESH,
            ).start()
            if before is not None:
                pltpu.make_async_copy(whole, whole, d_recv.at[before[0], before[1]]).wait()
                attend([(before[0], 1 - core, before[1]), (w, core, g)])
            else:
                attend([(w, core, g)])
            before = (w, g)
    pltpu.make_async_copy(whole, whole, d_recv.at[before[0], before[1]]).wait()
    attend([(before[0], 1 - core, before[1])], last=True)

    pltpu.make_async_copy(landed.at[pl.ds(0, NZ - 1)], landed.at[pl.ds(0, NZ - 1)], a_send).wait()
    for w in range(WAVES):
        sent = kv.at[w, 0, pl.ds(1, NX * NY - 1)]
        pltpu.make_async_copy(sent, sent, p_send.at[w]).wait()
    pltpu.make_async_copy(kv.at[:, 0], kv.at[:, 0], d_send).wait()


def shards(cand_queries, candidate_keys, candidate_values, prefix_keys, prefix_values, lengths):
    bf16, f32 = jnp.bfloat16, jnp.float32
    anywhere = pl.BlockSpec(memory_space=pl.ANY)
    dma = pltpu.SemaphoreType.DMA
    return pl.pallas_call(
        kernel,
        out_shape=pltpu.VMEM(cand_queries.shape, bf16),
        in_specs=[anywhere] * 6 + [pl.BlockSpec(memory_space=pltpu.SMEM)],
        out_specs=pl.BlockSpec(memory_space=pltpu.VMEM),
        scratch_shapes=[
            pltpu.VMEM(prefix_keys.shape, bf16),
            pltpu.VMEM(prefix_values.shape, bf16),
            pltpu.VMEM(cand_queries.shape, bf16),
            pltpu.VMEM(candidate_keys.shape, bf16),
            pltpu.VMEM(candidate_values.shape, bf16),
            pltpu.VMEM((SLOTS, HEAD_WIDTH), f32),
            pltpu.VMEM((KEY_VALUE_HEADS, 8, HEAD_WIDTH), bf16),
            pltpu.VMEM((NZ, 8, HEAD_WIDTH), bf16),
            pltpu.VMEM((WAVES, 2, NX * NY, 2, PER * 4, HEAD_WIDTH), bf16),
            pltpu.VMEM((ROWS, 2 * HEAD_WIDTH), f32),
            pltpu.VMEM((ROWS, HEAD_WIDTH), f32),
            dma((6,)),
            dma,
            dma((WAVES,)),
            dma((WAVES,)),
            dma((WAVES, SETS)),
            dma,
            dma((WAVES, SETS)),
            pltpu.SemaphoreType.REGULAR,
            pltpu.SemaphoreType.REGULAR,
            pltpu.SemaphoreType.REGULAR,
        ],
        compiler_params=pltpu.CompilerParams(
            collective_id=0, has_side_effects=True, vmem_limit_bytes=60 * 1024 * 1024
        ),
    )(prefix_keys, prefix_values, cand_queries, candidate_keys, candidate_values, jnp.asarray(rotation_table()), lengths)


def solution(mesh):
    split = P(("grp", "seq"), None, None)
    rows = P(("grp", "seq"), None)
    return jax.shard_map(
        shards,
        mesh=mesh,
        in_specs=(split, split, split, rows, rows, P()),
        out_specs=split,
        check_vma=False,
    )
```

time: 47.8 us -> 36.6 us (0.77)
  Pallas kernels: 41.3 us -> 35.5 us
  local copies, waits for them, and re-layouts: 6.06 us -> 0.71 us
    pallas_call x1, Pallas kernels: 41.3 us -> 35.5 us  [shards(): pl.pallas_call(kernel, out_shape=pltpu.VMEM(cand_queries.shape, bf16), in...]
    unnamed x15 -> x1, local copies, waits for them, and re-layouts: 6.06 us -> 0.71 us
where the time goes in v2:
time: 36.6 us; the launch traced here: 36.3 us
  Pallas kernels  35.5 us (97%)
  local copies, waits for them, and re-layouts  0.71 us (2%)
    pallas_call x1, Pallas kernels, shards(): pl.pallas_call(kernel, out_shape=pltpu.VMEM(cand_queries.shape, bf16), in...  35.5 us

profile of v2, /device:TPU:1, one launch (start us, length us, event | category | flops | bytes accessed | tf_op | source)
XLA Modules:
  0.0 36.3 jit_solution(2001566733349230800)
XLA Ops:
  0.0 35.5 %shard_map.73 = bf16[8,128,128]{2,1,0:T(8,128)(2,1)S(1)} custom-call(bf16[4,1024]{1,0:T(4,128)(2,1)} %kp_hbm.1, bf16[4,1024]{1,0:T(4,128)(2,1)} %vp_hbm.1, bf16[8,128,128]{2,1,0:T(8,128)(2,1)} %q_hbm.1, bf16[1,128,128]{2,1,0:T(8,128)(2,1)} %ck_hbm.1, bf16[1,128,128]{2,1,0:T(8,128)(2,1)} %cv_hbm.1, f32[128,128]{1,0:T(8,128)} %constant.2.clone.table_hbm, ...), custom_call_target="tpu_custom_call" | custom-call | tf_op jit(solution)/shard_map/pallas_call | solution.py:283
  35.5 0.7 %copy.9 = bf16[8,128,128]{2,1,0:T(8,128)(2,1)} copy(bf16[8,128,128]{2,1,0:T(8,128)(2,1)S(1)} %shard_map.73) | data formatting | bytes 524288

commit v3 on v2

--- a/solution.py
+++ b/solution.py
@@ -21,13 +21,12 @@
 
 NX, NY, NZ, ZL = 4, 4, 16, 8
 MESH = pl.DeviceIdType.MESH
-BLOCK = 256
 WAVES = 2
-EARLY, LATE = 4, 8
+EARLY, LATE = 5, 8
 PER = NZ // WAVES
 OFFSETS = sorted(
     [(dx, dy) for dx in range(NX) for dy in range(NY)],
-    key=lambda o: min(o[0], NX - o[0]) + min(o[1], NY - o[1]),
+    key=lambda o: -(min(o[0], NX - o[0]) + min(o[1], NY - o[1])) if any(o) else -99,
 )
 SET = 8
 SETS = NX * NY // SET
@@ -116,7 +115,7 @@
 
     @pl.when(core == 0)
     def _():
-        for dx, dy in OFFSETS[:0:-1]:
+        for dx, dy in OFFSETS[1:]:
             signal(barrier, (x + dx) % NX, (y + dy) % NY, z, 0)
         for zt in range(NZ):
             far_end = z != zt
@@ -147,19 +146,19 @@
         jnp.int32, (SLOTS, SLOTS), 0
     )
 
-    def own(h, carry):
+    def own(h):
         rows = rotate(q[h])
         q[h] = rows
         s = lax.dot_general(rows, new_keys, (((1,), (1,)), ((), ())), preferred_element_type=jnp.float32)
         s = jnp.where(causal, s * SCALE2, -jnp.inf)
         m = jnp.max(s, axis=1, keepdims=True)
         p = jnp.exp2(s - m).astype(jnp.bfloat16)
-        r = pl.ds(pl.multiple_of(h * SLOTS, SLOTS), SLOTS)
+        r = pl.ds(h * SLOTS, SLOTS)
         acc[r, :] = jnp.dot(p, new_values, preferred_element_type=jnp.float32)
         top[r, :] = jnp.broadcast_to(m, (SLOTS, HEAD_WIDTH))
-        return carry
-
-    lax.fori_loop(0, GROUP, own, 0)
+
+    for h in range(GROUP):
+        own(h)
 
     @pl.when(core == 0)
     def _():
@@ -212,40 +211,32 @@
                 for zt in range(LATE, NZ):
                     give(zt)
 
-    ones_block = jnp.ones((SET * PER * 4, HEAD_WIDTH), jnp.bfloat16)
+    keys_here = SET * PER * 4
+    ones_block = jnp.ones((keys_here, HEAD_WIDTH), jnp.bfloat16)
     mine = (grp * lax.axis_size("seq") + seq) // KEY_VALUE_HEADS
 
-    def attend(parts, last=False):
-        def rows_of(w, c, g, which):
-            return kv[w, c, g * SET : (g + 1) * SET, which].reshape(SET * PER * 4, HEAD_WIDTH)
-
-        def body(i, carry):
-            r = pl.ds(pl.multiple_of(i * BLOCK, BLOCK), BLOCK)
-            heads = BLOCK // SLOTS
-            rows = q[pl.ds(i * heads, heads)].reshape(BLOCK, HEAD_WIDTH)
-            keys = jnp.concatenate([rows_of(*p, 0) for p in parts], axis=0)
-            values = jnp.concatenate(
-                [jnp.concatenate([rows_of(*p, 1), ones_block], axis=1) for p in parts], axis=0
-            )
-            s = lax.dot_general(rows, keys, (((1,), (1,)), ((), ())), preferred_element_type=jnp.float32)
-            s = s * SCALE2
-            old = top[r, :]
-            m = jnp.maximum(old, jnp.max(s, axis=1, keepdims=True))
-            decline = jnp.exp2(old - m)
-            p = jnp.exp2(s - m[:, :1]).astype(jnp.bfloat16)
-            o = acc[r, :] * jnp.concatenate([decline, decline], axis=1) + jnp.dot(
-                p, values, preferred_element_type=jnp.float32
-            )
-            if not last:
-                acc[r, :] = o
-                top[r, :] = m
-            else:
-                token = lax.broadcasted_iota(jnp.int32, (BLOCK, HEAD_WIDTH), 0) % SLOTS
-                result = jnp.where(token < len_ref[mine], o[:, :HEAD_WIDTH] / o[:, HEAD_WIDTH:], 0.0)
-                out_ref[pl.ds(i * heads, heads)] = result.astype(jnp.bfloat16).reshape(heads, SLOTS, HEAD_WIDTH)
-            return carry
-
-        lax.fori_loop(0, ROWS // BLOCK, body, 0)
+    def attend(w, c, g, last=False):
+        block = kv[w, c, g * SET : (g + 1) * SET]
+        keys = block[:, 0].reshape(keys_here, HEAD_WIDTH)
+        values = jnp.concatenate([block[:, 1].reshape(keys_here, HEAD_WIDTH), ones_block], axis=1)
+        s = lax.dot_general(
+            q[...].reshape(ROWS, HEAD_WIDTH), keys, (((1,), (1,)), ((), ())), preferred_element_type=jnp.float32
+        )
+        tiles = [s[:, t : t + HEAD_WIDTH] for t in range(0, keys_here, HEAD_WIDTH)]
+        old = top[...]
+        m = jnp.maximum(old, jnp.max(functools.reduce(jnp.maximum, tiles), axis=1, keepdims=True) * SCALE2)
+        decline = jnp.exp2(old - m)
+        p = jnp.concatenate([jnp.exp2(t * SCALE2 - m).astype(jnp.bfloat16) for t in tiles], axis=1)
+        o = acc[...] * jnp.concatenate([decline, decline], axis=1) + jnp.dot(
+            p, values, preferred_element_type=jnp.float32
+        )
+        if not last:
+            acc[...] = o
+            top[...] = m
+        else:
+            token = lax.broadcasted_iota(jnp.int32, (ROWS, HEAD_WIDTH), 0) % SLOTS
+            result = jnp.where(token < len_ref[mine], o[:, :HEAD_WIDTH] / o[:, HEAD_WIDTH:], 0.0)
+            out_ref[...] = result.astype(jnp.bfloat16).reshape(GROUP, SLOTS, HEAD_WIDTH)
 
     before = None
     for w in range(WAVES):
@@ -262,12 +253,11 @@
             ).start()
             if before is not None:
                 pltpu.make_async_copy(whole, whole, d_recv.at[before[0], before[1]]).wait()
-                attend([(before[0], 1 - core, before[1]), (w, core, g)])
-            else:
-                attend([(w, core, g)])
+                attend(before[0], 1 - core, before[1])
+            attend(w, core, g)
             before = (w, g)
     pltpu.make_async_copy(whole, whole, d_recv.at[before[0], before[1]]).wait()
-    attend([(before[0], 1 - core, before[1])], last=True)
+    attend(before[0], 1 - core, before[1], last=True)
 
     pltpu.make_async_copy(landed.at[pl.ds(0, NZ - 1)], landed.at[pl.ds(0, NZ - 1)], a_send).wait()
     for w in range(WAVES):

time: 36.6 us -> 30.3 us (0.83)
  Pallas kernels: 35.5 us -> 29.5 us
    pallas_call x1, Pallas kernels: 35.5 us -> 29.5 us  [shards(): pl.pallas_call(kernel, out_shape=pltpu.VMEM(cand_queries.shape, bf16), in...]
where the time goes in v3:
time: 30.3 us; the launch traced here: 30.2 us
  Pallas kernels  29.5 us (97%)
  local copies, waits for them, and re-layouts  0.71 us (2%)
    pallas_call x1, Pallas kernels, shards(): pl.pallas_call(kernel, out_shape=pltpu.VMEM(cand_queries.shape, bf16), in...  29.5 us
    unnamed x1, local copies, waits for them, and re-layouts  0.71 us

profile of v3, /device:TPU:1, one launch (start us, length us, event | category | flops | bytes accessed | tf_op | source)
XLA Modules:
  0.0 30.2 jit_solution(16538683611122664979)
XLA Ops:
  0.0 29.5 %shard_map.73 = bf16[8,128,128]{2,1,0:T(8,128)(2,1)S(1)} custom-call(bf16[4,1024]{1,0:T(4,128)(2,1)} %kp_hbm.1, bf16[4,1024]{1,0:T(4,128)(2,1)} %vp_hbm.1, bf16[8,128,128]{2,1,0:T(8,128)(2,1)} %q_hbm.1, bf16[1,128,128]{2,1,0:T(8,128)(2,1)} %ck_hbm.1, bf16[1,128,128]{2,1,0:T(8,128)(2,1)} %cv_hbm.1, f32[128,128]{1,0:T(8,128)} %constant.2.clone.table_hbm, ...), custom_call_target="tpu_custom_call" | custom-call | tf_op jit(solution)/shard_map/pallas_call | solution.py:273
  29.5 0.7 %copy.9 = bf16[8,128,128]{2,1,0:T(8,128)(2,1)} copy(bf16[8,128,128]{2,1,0:T(8,128)(2,1)S(1)} %shard_map.73) | data formatting | bytes 524288

commit v4 on v3

--- a/solution.py
+++ b/solution.py
@@ -21,15 +21,13 @@
 
 NX, NY, NZ, ZL = 4, 4, 16, 8
 MESH = pl.DeviceIdType.MESH
-WAVES = 2
-EARLY, LATE = 5, 8
+WAVES = 4
+EARLY, LATE = 4, 8
 PER = NZ // WAVES
 OFFSETS = sorted(
     [(dx, dy) for dx in range(NX) for dy in range(NY)],
     key=lambda o: -(min(o[0], NX - o[0]) + min(o[1], NY - o[1])) if any(o) else -99,
 )
-SET = 8
-SETS = NX * NY // SET
 
 
 def rotation_table():
@@ -47,7 +45,7 @@
 
 def kernel(
     kp_hbm, vp_hbm, q_hbm, ck_hbm, cv_hbm, table_hbm, len_ref, out_ref,
-    kp, vp, q, ck, cv, table, send, landed, kv, acc, top,
+    q, ck, cv, table, landed, kv, acc, top,
     in_sem, a_send, a_recv, p_send, p_recv, d_send, d_recv, ready, late_in, all_in,
 ):
     grp, seq = lax.axis_index("grp"), lax.axis_index("seq")
@@ -59,7 +57,7 @@
     loads = [
         pltpu.make_async_copy(s, d, in_sem.at[i])
         for i, (s, d) in enumerate(
-            [(kp_hbm, kp), (vp_hbm, vp), (q_hbm, q), (ck_hbm, ck), (cv_hbm, cv), (table_hbm, table)]
+            [(q_hbm, q), (ck_hbm, ck), (cv_hbm, cv), (table_hbm, table)]
         )
     ]
     for load in loads:
@@ -75,33 +73,28 @@
 
         @pl.when(early & (z != zt))
         def _():
-            signal(barrier, x, y, zt, 1)
+            signal(barrier, x, y, zt, 0)
+
+    @pl.when(core == 1)
+    def _():
+        signal(barrier, x, y, z, 0)
 
     @pl.when(core == 0)
     def _():
-        signal(barrier, x, y, z, 1)
-
-    loads[0].wait()
-    loads[1].wait()
-    both = jnp.concatenate([kp[...].astype(jnp.float32), vp[...].astype(jnp.float32)], axis=0)
-    both = both.astype(jnp.bfloat16)
-    for h in range(KEY_VALUE_HEADS):
-        send[h] = both[:, h * HEAD_WIDTH : (h + 1) * HEAD_WIDTH]
+        pl.semaphore_wait(barrier, jnp.where(early, 2 * EARLY - 1, 2 * EARLY + 1))
+        signal(ready, x, y, z, 1)
 
     @pl.when(core == 1)
     def _():
-        pl.semaphore_wait(barrier, jnp.where(early, 2 * EARLY - 1, 2 * EARLY + 1))
-        signal(ready, x, y, z, 0)
-
-    @pl.when(core == 0)
-    def _():
         pl.semaphore_wait(ready, 1)
 
     def give(zt):
-        pltpu.make_async_remote_copy(
-            src_ref=send.at[zt % ZL], dst_ref=landed.at[z], send_sem=a_send, recv_sem=a_recv.at[z // PER],
-            device_id=device(x, y, zt, core), device_id_type=MESH,
-        ).start()
+        head = pl.ds(zt % ZL * HEAD_WIDTH, HEAD_WIDTH)
+        for i, ref in enumerate((kp_hbm, vp_hbm)):
+            pltpu.make_async_remote_copy(
+                src_ref=ref.at[:, head], dst_ref=landed.at[z, i], send_sem=a_send, recv_sem=a_recv.at[z // PER],
+                device_id=device(x, y, zt, core), device_id_type=MESH,
+            ).start()
 
     for zt in range(EARLY):
 
@@ -109,14 +102,16 @@
         def _():
             give(zt)
 
+    for zt in range(EARLY):
+
         @pl.when(late)
         def _():
             signal(late_in, x, y, zt, core)
 
-    @pl.when(core == 0)
+    @pl.when(core == 1)
     def _():
         for dx, dy in OFFSETS[1:]:
-            signal(barrier, (x + dx) % NX, (y + dy) % NY, z, 0)
+            signal(barrier, (x + dx) % NX, (y + dy) % NY, z, 1)
         for zt in range(NZ):
             far_end = z != zt
             if zt < EARLY:
@@ -124,9 +119,13 @@
 
             @pl.when(far_end & ~early)
             def _():
-                signal(barrier, x, y, zt, 0)
-
-    for load in loads[2:]:
+                signal(barrier, x, y, zt, 1)
+
+    head = pl.ds(pl.multiple_of(z % ZL * HEAD_WIDTH, HEAD_WIDTH), HEAD_WIDTH)
+    for i, ref in enumerate((kp_hbm, vp_hbm)):
+        pltpu.make_async_copy(ref.at[:, head], landed.at[z, i], a_recv.at[z // PER]).start()
+
+    for load in loads:
         load.wait()
     lower = lax.broadcasted_iota(jnp.int32, (SLOTS, HEAD_WIDTH), 1) < HEAD_WIDTH // 2
     cs = table[...]
@@ -160,14 +159,14 @@
     for h in range(GROUP):
         own(h)
 
-    @pl.when(core == 0)
+    @pl.when(core == 1)
     def _():
         plane, middle = NX * NY - 1, LATE - EARLY
         others = jnp.where(early, middle, NZ - EARLY - 1)
         pl.semaphore_wait(barrier, plane + others)
-        signal(all_in, x, y, z, 1)
-
-    @pl.when(core == 1)
+        signal(all_in, x, y, z, 0)
+
+    @pl.when(core == 0)
     def _():
         pl.semaphore_wait(all_in, 1)
 
@@ -180,30 +179,38 @@
         def _():
             give(zt)
 
-    pltpu.make_async_copy(send.at[z % ZL], landed.at[z], a_recv.at[z // PER]).start()
-
-    half_line = lax.broadcasted_iota(jnp.int32, (8, HEAD_WIDTH), 0) < 4
+    def quarter(w):
+        own = z // PER
+        near = jnp.where(z < 2, (0, 3, 1, 2)[w], (0, 1, 3, 2)[w])
+        far = (own, 5 - own, 0, 1)[w]
+        return jnp.where(early, near, jnp.where(z < NZ // 2, (0, 1, 3, 2)[w], far))
+
+    place = x * NY + y
     for w in range(WAVES):
-        src = (z // PER + w) % WAVES
+        src = quarter(w)
         arrived = landed.at[pl.ds(src * PER, PER)]
         pltpu.make_async_copy(arrived, arrived, a_recv.at[src]).wait()
-        keys, values = [], []
-        for i in range(0, PER, 2):
-            even = landed[src * PER + i].astype(jnp.float32)
-            odd = landed[src * PER + i + 1].astype(jnp.float32)
-            keys.append(jnp.where(half_line, even, pltpu.roll(odd, 4, 0)))
-            values.append(jnp.where(half_line, pltpu.roll(even, 4, 0), odd))
-        kv[w, core, 0, 0] = jnp.concatenate(keys, axis=0).astype(jnp.bfloat16)
-        kv[w, core, 0, 1] = jnp.concatenate(values, axis=0).astype(jnp.bfloat16)
-        for i, (dx, dy) in enumerate(OFFSETS):
-            if i:
-                pltpu.make_async_remote_copy(
-                    src_ref=kv.at[w, core, 0], dst_ref=kv.at[w, core, i], send_sem=p_send.at[w],
-                    recv_sem=p_recv.at[w, i // SET], device_id=device((x + dx) % NX, (y + dy) % NY, z, core),
-                    device_id_type=MESH,
-                ).start()
-
-        if w == 0:
+        for which in (0, 1):
+            rows = [landed[src * PER + i, which].astype(jnp.float32) for i in range(PER)]
+            kv[w, core, place, which] = jnp.concatenate(rows, axis=0).astype(jnp.bfloat16)
+        def pass_on(tx, ty):
+            pltpu.make_async_remote_copy(
+                src_ref=kv.at[w, core, place], dst_ref=kv.at[w, core, place], send_sem=p_send.at[w],
+                recv_sem=p_recv.at[w], device_id=device(tx, ty, z, core), device_id_type=MESH,
+            ).start()
+
+        @pl.when(place != 0)
+        def _():
+            pass_on(0, 0)
+
+        for dx, dy in OFFSETS[1:]:
+            tx, ty = (x + dx) % NX, (y + dy) % NY
+
+            @pl.when(tx + ty != 0)
+            def _():
+                pass_on(tx, ty)
+
+        if w == 1:
 
             @pl.when(early)
             def _():
@@ -211,12 +218,12 @@
                 for zt in range(LATE, NZ):
                     give(zt)
 
-    keys_here = SET * PER * 4
+    keys_here = NX * NY * PER * 4
     ones_block = jnp.ones((keys_here, HEAD_WIDTH), jnp.bfloat16)
     mine = (grp * lax.axis_size("seq") + seq) // KEY_VALUE_HEADS
 
-    def attend(w, c, g, last=False):
-        block = kv[w, c, g * SET : (g + 1) * SET]
+    def attend(w, c, last=False):
+        block = kv[w, c]
         keys = block[:, 0].reshape(keys_here, HEAD_WIDTH)
         values = jnp.concatenate([block[:, 1].reshape(keys_here, HEAD_WIDTH), ones_block], axis=1)
         s = lax.dot_general(
@@ -238,30 +245,26 @@
             result = jnp.where(token < len_ref[mine], o[:, :HEAD_WIDTH] / o[:, HEAD_WIDTH:], 0.0)
             out_ref[...] = result.astype(jnp.bfloat16).reshape(GROUP, SLOTS, HEAD_WIDTH)
 
-    before = None
+    peers = NX * NY - 1
     for w in range(WAVES):
-        for g in range(SETS):
-            whole = kv.at[w, core, pl.ds(g * SET, SET)]
-            if g:
-                pltpu.make_async_copy(whole, whole, p_recv.at[w, g]).wait()
-            else:
-                rest = kv.at[w, core, pl.ds(1, SET - 1)]
-                pltpu.make_async_copy(rest, rest, p_recv.at[w, g]).wait()
-            pltpu.make_async_remote_copy(
-                src_ref=whole, dst_ref=whole, send_sem=d_send, recv_sem=d_recv.at[w, g],
-                device_id=device(x, y, z, 1 - core), device_id_type=MESH,
-            ).start()
-            if before is not None:
-                pltpu.make_async_copy(whole, whole, d_recv.at[before[0], before[1]]).wait()
-                attend(before[0], 1 - core, before[1])
-            attend(w, core, g)
-            before = (w, g)
-    pltpu.make_async_copy(whole, whole, d_recv.at[before[0], before[1]]).wait()
-    attend(before[0], 1 - core, before[1], last=True)
-
-    pltpu.make_async_copy(landed.at[pl.ds(0, NZ - 1)], landed.at[pl.ds(0, NZ - 1)], a_send).wait()
+        rest = kv.at[w, core, pl.ds(0, peers)]
+        pltpu.make_async_copy(rest, rest, p_recv.at[w]).wait()
+        whole = kv.at[w, core]
+        pltpu.make_async_remote_copy(
+            src_ref=whole, dst_ref=whole, send_sem=d_send, recv_sem=d_recv.at[w],
+            device_id=device(x, y, z, 1 - core), device_id_type=MESH,
+        ).start()
+        if w:
+            pltpu.make_async_copy(whole, whole, d_recv.at[w - 1]).wait()
+            attend(w - 1, 1 - core)
+        attend(w, core)
+    pltpu.make_async_copy(whole, whole, d_recv.at[WAVES - 1]).wait()
+    attend(WAVES - 1, 1 - core, last=True)
+
+    given = landed.at[pl.ds(0, NZ - 1)]
+    pltpu.make_async_copy(given, given, a_send).wait()
     for w in range(WAVES):
-        sent = kv.at[w, 0, pl.ds(1, NX * NY - 1)]
+        sent = kv.at[w, 0, pl.ds(0, peers)]
         pltpu.make_async_copy(sent, sent, p_send.at[w]).wait()
     pltpu.make_async_copy(kv.at[:, 0], kv.at[:, 0], d_send).wait()
 
@@ -276,24 +279,21 @@
         in_specs=[anywhere] * 6 + [pl.BlockSpec(memory_space=pltpu.SMEM)],
         out_specs=pl.BlockSpec(memory_space=pltpu.VMEM),
         scratch_shapes=[
-            pltpu.VMEM(prefix_keys.shape, bf16),
-            pltpu.VMEM(prefix_values.shape, bf16),
             pltpu.VMEM(cand_queries.shape, bf16),
             pltpu.VMEM(candidate_keys.shape, bf16),
             pltpu.VMEM(candidate_values.shape, bf16),
             pltpu.VMEM((SLOTS, HEAD_WIDTH), f32),
-            pltpu.VMEM((KEY_VALUE_HEADS, 8, HEAD_WIDTH), bf16),
-            pltpu.VMEM((NZ, 8, HEAD_WIDTH), bf16),
+            pltpu.VMEM((NZ, 2, 4, HEAD_WIDTH), bf16),
             pltpu.VMEM((WAVES, 2, NX * NY, 2, PER * 4, HEAD_WIDTH), bf16),
             pltpu.VMEM((ROWS, 2 * HEAD_WIDTH), f32),
             pltpu.VMEM((ROWS, HEAD_WIDTH), f32),
-            dma((6,)),
+            dma((4,)),
             dma,
             dma((WAVES,)),
             dma((WAVES,)),
-            dma((WAVES, SETS)),
+            dma((WAVES,)),
             dma,
-            dma((WAVES, SETS)),
+            dma((WAVES,)),
             pltpu.SemaphoreType.REGULAR,
             pltpu.SemaphoreType.REGULAR,
             pltpu.SemaphoreType.REGULAR,

time: 30.3 us -> 28.6 us (0.944)
  Pallas kernels: 29.5 us -> 27.8 us
    pallas_call x1, Pallas kernels: 29.5 us -> 27.8 us  [shards(): pl.pallas_call(kernel, out_shape=pltpu.VMEM(cand_queries.shape, bf16), in...]
where the time goes in v4:
time: 28.6 us; the launch traced here: 28.5 us
  Pallas kernels  27.8 us (97%)
  local copies, waits for them, and re-layouts  0.71 us (2%)
    pallas_call x1, Pallas kernels, shards(): pl.pallas_call(kernel, out_shape=pltpu.VMEM(cand_queries.shape, bf16), in...  27.8 us
    unnamed x1, local copies, waits for them, and re-layouts  0.71 us

profile of v4, /device:TPU:1, one launch (start us, length us, event | category | flops | bytes accessed | tf_op | source)
XLA Modules:
  0.0 28.5 jit_solution(10347822650818550042)
XLA Ops:
  0.0 27.8 %shard_map.73 = bf16[8,128,128]{2,1,0:T(8,128)(2,1)S(1)} custom-call(bf16[4,1024]{1,0:T(4,128)(2,1)} %kp_hbm.1, bf16[4,1024]{1,0:T(4,128)(2,1)} %vp_hbm.1, bf16[8,128,128]{2,1,0:T(8,128)(2,1)} %q_hbm.1, bf16[1,128,128]{2,1,0:T(8,128)(2,1)} %ck_hbm.1, bf16[1,128,128]{2,1,0:T(8,128)(2,1)} %cv_hbm.1, f32[128,128]{1,0:T(8,128)} %constant.2.clone.table_hbm, ...), custom_call_target="tpu_custom_call" | custom-call | tf_op jit(solution)/shard_map/pallas_call | solution.py:276
  27.8 0.7 %copy.9 = bf16[8,128,128]{2,1,0:T(8,128)(2,1)} copy(bf16[8,128,128]{2,1,0:T(8,128)(2,1)S(1)} %shard_map.73) | data formatting | bytes 524288

commit v5 on v4

--- a/solution.py
+++ b/solution.py
@@ -46,7 +46,7 @@
 def kernel(
     kp_hbm, vp_hbm, q_hbm, ck_hbm, cv_hbm, table_hbm, len_ref, out_ref,
     q, ck, cv, table, landed, kv, acc, top,
-    in_sem, a_send, a_recv, p_send, p_recv, d_send, d_recv, ready, late_in, all_in,
+    in_sem, a_send, a_recv, p_send, p_recv, d_send, d_recv, e_send, ready, late_in, all_in,
 ):
     grp, seq = lax.axis_index("grp"), lax.axis_index("seq")
     core, zh = grp % 2, grp // 2
@@ -181,7 +181,7 @@
 
     def quarter(w):
         own = z // PER
-        near = jnp.where(z < 2, (0, 3, 1, 2)[w], (0, 1, 3, 2)[w])
+        near = (0, 1, 3, 2)[w]
         far = (own, 5 - own, 0, 1)[w]
         return jnp.where(early, near, jnp.where(z < NZ // 2, (0, 1, 3, 2)[w], far))
 
@@ -198,6 +198,16 @@
                 src_ref=kv.at[w, core, place], dst_ref=kv.at[w, core, place], send_sem=p_send.at[w],
                 recv_sem=p_recv.at[w], device_id=device(tx, ty, z, core), device_id_type=MESH,
             ).start()
+            if w == WAVES - 1:
+                pass_across(tx, ty)
+
+        def pass_across(tx, ty):
+            @pl.when(core == 0)
+            def _():
+                pltpu.make_async_remote_copy(
+                    src_ref=kv.at[w, 0, place], dst_ref=kv.at[w, 0, place], send_sem=e_send,
+                    recv_sem=d_recv.at[w], device_id=device(tx, ty, z, 1), device_id_type=MESH,
+                ).start()
 
         @pl.when(place != 0)
         def _():
@@ -209,6 +219,9 @@
             @pl.when(tx + ty != 0)
             def _():
                 pass_on(tx, ty)
+
+        if w == WAVES - 1:
+            pass_across(x, y)
 
         if w == 1:
 
@@ -250,10 +263,20 @@
         rest = kv.at[w, core, pl.ds(0, peers)]
         pltpu.make_async_copy(rest, rest, p_recv.at[w]).wait()
         whole = kv.at[w, core]
-        pltpu.make_async_remote_copy(
-            src_ref=whole, dst_ref=whole, send_sem=d_send, recv_sem=d_recv.at[w],
-            device_id=device(x, y, z, 1 - core), device_id_type=MESH,
-        ).start()
+        if w < WAVES - 1:
+            pltpu.make_async_remote_copy(
+                src_ref=whole, dst_ref=whole, send_sem=d_send, recv_sem=d_recv.at[w],
+                device_id=device(x, y, z, 1 - core), device_id_type=MESH,
+            ).start()
+        else:
+
+            @pl.when(core == 1)
+            def _():
+                pltpu.make_async_remote_copy(
+                    src_ref=kv.at[w, 1], dst_ref=kv.at[w, 1], send_sem=e_send, recv_sem=d_recv.at[w],
+                    device_id=device(x, y, z, 0), device_id_type=MESH,
+                ).start()
+
         if w:
             pltpu.make_async_copy(whole, whole, d_recv.at[w - 1]).wait()
             attend(w - 1, 1 - core)
@@ -266,7 +289,9 @@
     for w in range(WAVES):
         sent = kv.at[w, 0, pl.ds(0, peers)]
         pltpu.make_async_copy(sent, sent, p_send.at[w]).wait()
-    pltpu.make_async_copy(kv.at[:, 0], kv.at[:, 0], d_send).wait()
+    before = kv.at[pl.ds(0, WAVES - 1), 0]
+    pltpu.make_async_copy(before, before, d_send).wait()
+    pltpu.make_async_copy(whole, whole, e_send).wait()
 
 
 def shards(cand_queries, candidate_keys, candidate_values, prefix_keys, prefix_values, lengths):
@@ -294,6 +319,7 @@
             dma((WAVES,)),
             dma,
             dma((WAVES,)),
+            dma,
             pltpu.SemaphoreType.REGULAR,
             pltpu.SemaphoreType.REGULAR,
             pltpu.SemaphoreType.REGULAR,

time: 28.6 us -> 28.3 us (0.990)
  Pallas kernels: 27.8 us -> 27.4 us
    pallas_call x1, Pallas kernels: 27.8 us -> 27.4 us  [shards(): pl.pallas_call(kernel, out_shape=pltpu.VMEM(cand_queries.shape, bf16), in...]
where the time goes in v5:
time: 28.3 us; the launch traced here: 28.1 us
  Pallas kernels  27.4 us (97%)
  local copies, waits for them, and re-layouts  0.71 us (3%)
    pallas_call x1, Pallas kernels, shards(): pl.pallas_call(kernel, out_shape=pltpu.VMEM(cand_queries.shape, bf16), in...  27.4 us
    unnamed x1, local copies, waits for them, and re-layouts  0.71 us

profile of v5, /device:TPU:1, one launch (start us, length us, event | category | flops | bytes accessed | tf_op | source)
XLA Modules:
  0.0 28.1 jit_solution(12528018210328430704)
XLA Ops:
  0.0 27.4 %shard_map.73 = bf16[8,128,128]{2,1,0:T(8,128)(2,1)S(1)} custom-call(bf16[4,1024]{1,0:T(4,128)(2,1)} %kp_hbm.1, bf16[4,1024]{1,0:T(4,128)(2,1)} %vp_hbm.1, bf16[8,128,128]{2,1,0:T(8,128)(2,1)} %q_hbm.1, bf16[1,128,128]{2,1,0:T(8,128)(2,1)} %ck_hbm.1, bf16[1,128,128]{2,1,0:T(8,128)(2,1)} %cv_hbm.1, f32[128,128]{1,0:T(8,128)} %constant.2.clone.table_hbm, ...), custom_call_target="tpu_custom_call" | custom-call | tf_op jit(solution)/shard_map/pallas_call | solution.py:301
  27.4 0.7 %copy.9 = bf16[8,128,128]{2,1,0:T(8,128)(2,1)} copy(bf16[8,128,128]{2,1,0:T(8,128)(2,1)S(1)} %shard_map.73) | data formatting | bytes 524288

commit v6 on v5

--- a/solution.py
+++ b/solution.py
@@ -183,7 +183,7 @@
         own = z // PER
         near = (0, 1, 3, 2)[w]
         far = (own, 5 - own, 0, 1)[w]
-        return jnp.where(early, near, jnp.where(z < NZ // 2, (0, 1, 3, 2)[w], far))
+        return jnp.where(early, near, jnp.where(z < NZ // 2, (0, 1, 2, 3)[w], far))
 
     place = x * NY + y
     for w in range(WAVES):
@@ -194,12 +194,12 @@
             rows = [landed[src * PER + i, which].astype(jnp.float32) for i in range(PER)]
             kv[w, core, place, which] = jnp.concatenate(rows, axis=0).astype(jnp.bfloat16)
         def pass_on(tx, ty):
+            if w == WAVES - 1:
+                pass_across(tx, ty)
             pltpu.make_async_remote_copy(
                 src_ref=kv.at[w, core, place], dst_ref=kv.at[w, core, place], send_sem=p_send.at[w],
                 recv_sem=p_recv.at[w], device_id=device(tx, ty, z, core), device_id_type=MESH,
             ).start()
-            if w == WAVES - 1:
-                pass_across(tx, ty)
 
         def pass_across(tx, ty):
             @pl.when(core == 0)

time: 28.3 us -> 28.3 us (level)
  no operation moved by 1% of the time
where the time goes in v6:
time: 28.3 us; the launch traced here: 28.1 us
  Pallas kernels  27.4 us (97%)
  local copies, waits for them, and re-layouts  0.71 us (3%)
    pallas_call x1, Pallas kernels, shards(): pl.pallas_call(kernel, out_shape=pltpu.VMEM(cand_queries.shape, bf16), in...  27.4 us
    unnamed x1, local copies, waits for them, and re-layouts  0.71 us

profile of v6, /device:TPU:1, one launch (start us, length us, event | category | flops | bytes accessed | tf_op | source)
XLA Modules:
  0.0 28.1 jit_solution(11607701340722886555)
XLA Ops:
  0.0 27.4 %shard_map.73 = bf16[8,128,128]{2,1,0:T(8,128)(2,1)S(1)} custom-call(bf16[4,1024]{1,0:T(4,128)(2,1)} %kp_hbm.1, bf16[4,1024]{1,0:T(4,128)(2,1)} %vp_hbm.1, bf16[8,128,128]{2,1,0:T(8,128)(2,1)} %q_hbm.1, bf16[1,128,128]{2,1,0:T(8,128)(2,1)} %ck_hbm.1, bf16[1,128,128]{2,1,0:T(8,128)(2,1)} %cv_hbm.1, f32[128,128]{1,0:T(8,128)} %constant.2.clone.table_hbm, ...), custom_call_target="tpu_custom_call" | custom-call | tf_op jit(solution)/shard_map/pallas_call | solution.py:301
  27.4 0.7 %copy.9 = bf16[8,128,128]{2,1,0:T(8,128)(2,1)} copy(bf16[8,128,128]{2,1,0:T(8,128)(2,1)S(1)} %shard_map.73) | data formatting | bytes 524288
